TPU v7x, 256 devices: a whole 4x4x8 slice. The times are simulated.
256 devices in a mesh: fsdp: 16 (over z, core), slab: 8 (over y, x_lo), rep: 2 (over x_hi).
Axes of the slice: x: 4 (x_hi: 2, x_lo: 2; x = x_hi * 2 + x_lo), y: 4, z: 8, core: 2. Of those that a mesh axis runs over, the one named last changes fastest.
Arguments:
- inputs: bfloat16 [32, 32, 8, 8, 256], P(('fsdp', 'rep'), 'slab'), may hold values from -6 to 6
- weights: bfloat16 [256, 27, 256], P('fsdp'), may hold values from -0.078125 to 0.078125
- upstream: bfloat16 [32, 32, 8, 8, 256], P(('fsdp', 'rep'), 'slab'), may hold values from -6 to 6
Outputs:
- activated: bfloat16 [32, 32, 8, 8, 256], P(('fsdp', 'rep'), 'slab')
- input_grad: bfloat16 [32, 32, 8, 8, 256], P(('fsdp', 'rep'), 'slab')
- weight_grad: float32 [256, 27, 256], P('fsdp')
All inputs are finite; a program needn't handle non-finite values.
Results may differ from a plain program's by a relative error of at most 0.0049.
Values may be sent and summed in bfloat16 or wider, within the bound.
No kernel may reach another device: no remote copies, remote signals or barrier semaphores. Data moves between devices by JAX's collectives and lax.ppermute only.
A program may use at most 256 MiB of HBM per device.

v0:
```python
import jax
import jax.numpy as jnp
from jax import lax
from jax.sharding import PartitionSpec as P


def padded_2(cells, sides, width):
    for axis, dim in sides:
        count = lax.axis_size(axis)
        ends = count - 1
        head = lax.slice_in_dim(cells, 0, width, axis=dim)
        tail = lax.slice_in_dim(cells, cells.shape[dim] - width, cells.shape[dim], axis=dim)
        cells = jnp.concatenate(
            [
                lax.ppermute(tail, axis, [(i, (i + 1) % count) for i in range(ends)]),
                cells,
                lax.ppermute(head, axis, [((i + 1) % count, i) for i in range(ends)]),
            ],
            axis=dim,
        )
    return cells


def silu_slope(preact):
    logistic = jax.nn.sigmoid(preact)
    return logistic * (1.0 + preact * (1.0 - logistic))


def pad_cross(field):
    return jnp.pad(field, ((0, 0), (0, 0), (1, 1), (1, 1), (0, 0)))


def grad_rim(field):
    return pad_cross(padded_2(field, (("slab", 1),), 1))


def tap_list():
    return [
        (along_x, along_y, along_z)
        for along_x in range(3)
        for along_y in range(3)
        for along_z in range(3)
    ]


def forward_rows(padded, weight_rows):
    planes = padded.shape[1] - 2
    height = padded.shape[2] - 2
    breadth = padded.shape[3] - 2
    total = None
    for index, (along_x, along_y, along_z) in enumerate(tap_list()):
        window = padded[
            :,
            along_x : along_x + planes,
            along_y : along_y + height,
            along_z : along_z + breadth,
            :,
        ]
        term = jnp.einsum(
            "bxyzi,oi->bxyzo", window, weight_rows[:, index, :], preferred_element_type=jnp.float32
        )
        total = term if total is None else total + term
    return total


def backward_rows(grads_pad, weight_rows):
    planes = grads_pad.shape[1] - 2
    height = grads_pad.shape[2] - 2
    breadth = grads_pad.shape[3] - 2
    total = None
    for index, (along_x, along_y, along_z) in enumerate(tap_list()):
        grad_window = grads_pad[
            :,
            2 - along_x : 2 - along_x + planes,
            2 - along_y : 2 - along_y + height,
            2 - along_z : 2 - along_z + breadth,
            :,
        ]
        term = jnp.einsum(
            "bxyzo,oi->bxyzi",
            grad_window,
            weight_rows[:, index, :],
            preferred_element_type=jnp.float32,
        )
        total = term if total is None else total + term
    return total


def weight_terms(grads, padded, factor):
    planes = grads.shape[1]
    height = grads.shape[2]
    breadth = grads.shape[3]
    stacked = []
    for along_x, along_y, along_z in tap_list():
        window = padded[
            :,
            along_x : along_x + planes,
            along_y : along_y + height,
            along_z : along_z + breadth,
            :,
        ]
        stacked.append(
            jnp.einsum("bxyzo,bxyzi->oi", grads, window, preferred_element_type=jnp.float32)
        )
    return jnp.stack(stacked, axis=1) * factor


def local(inputs, weights, upstream):
    samples = inputs.shape[0]
    planes = inputs.shape[1]
    height = inputs.shape[2]
    breadth = inputs.shape[3]
    total_cells = (
        samples
        * lax.axis_size("fsdp")
        * lax.axis_size("rep")
        * planes
        * lax.axis_size("slab")
        * height
        * breadth
    )
    factor = float(total_cells) ** (-0.5)
    inputs_halo = padded_2(inputs, (("slab", 1),), 1)
    inputs_pad = pad_cross(inputs_halo)
    whole = lax.all_gather(weights, "fsdp", axis=0, tiled=True)
    preact = forward_rows(inputs_pad, whole)
    activated = jax.nn.silu(preact).astype(jnp.bfloat16)
    grad_pre = (upstream.astype(jnp.float32) * silu_slope(preact)).astype(jnp.bfloat16)
    grads_pad = grad_rim(grad_pre)
    input_grad = backward_rows(grads_pad, whole).astype(jnp.bfloat16)
    terms = weight_terms(grad_pre, inputs_pad, factor)
    shard = lax.psum_scatter(terms, "fsdp", scatter_dimension=0, tiled=True)
    weight_grad = lax.psum(shard, ("slab", "rep"))
    return (activated, input_grad, weight_grad)


def solution(mesh):
    placed = (
        P(("fsdp", "rep"), "slab", None, None, None),
        P("fsdp", None, None),
        P(("fsdp", "rep"), "slab", None, None, None),
    )
    return jax.shard_map(
        local,
        mesh=mesh,
        in_specs=placed,
        out_specs=(
            P(("fsdp", "rep"), "slab", None, None, None),
            P(("fsdp", "rep"), "slab", None, None, None),
            P("fsdp", None, None),
        ),
        check_vma=False,
    )
```

profile of v0, /device:TPU:32, one launch (start us, length us, event | category | flops | bytes accessed | tf_op | source)
XLA Modules:
  0.0 247.4 jit_solution(10040391627877063961)
XLA Ops:
  7.2 0.7 all-gather.2.cloned.1.call-update
  8.0 0.8 fusion.94
  8.7 3.4 %collective-permute-start = (bf16[1,1,8,8,256]{4,3,2,1,0:T(8,128)(2,1)S(1)}, bf16[1,1,8,8,256]{4,3,2,1,0:T(8,128)(2,1)S(1)}, u32[]{:S(2)}, u32[]{:S(2)}) collective-permute-start(bf16[1,1,8,8,256]{4,3,2,1,0:T(8,128)(2,1)S(1)} %get-tuple-element.5), channel_id=1, source_target_pairs={{0,2},{2,4},{4,6},{6,8},{8,10},{10,12},{12,14},{1,3},{3,5},{5,7},{... | collective-permute-start | bytes 98312 | tf_op jit(solution)/shard_map/ppermute | solution.py:15
  12.1 1.3 collective-permute-start.1
  13.4 0.3 collective-permute-done
  13.7 4.2 %collective-permute-done.1 = bf16[1,1,8,8,256]{4,3,2,1,0:T(8,128)(2,1)S(1)} collective-permute-done((bf16[1,1,8,8,256]{4,3,2,1,0:T(8,128)(2,1)S(1)}, bf16[1,1,8,8,256]{4,3,2,1,0:T(8,128)(2,1)S(1)}, u32[]{:S(2)}, u32[]{:S(2)}) %collective-permute-start.1) | collective-permute-done | bytes 32800 | tf_op jit(solution)/shard_map/ppermute | solution.py:17
  17.9 1.1 select_maximum_fusion.2
  19.0 34.5 %all-gather.2.cloned.1.call-done = bf16[256,27,256]{2,0,1:T(8,128)(2,1)} async-done(((bf16[16,27,256]{2,0,1:T(8,128)(2,1)}), bf16[256,27,256]{2,0,1:T(8,128)(2,1)}) %all-gather.2.cloned.1.call-update) | async-done | bytes 3538960 | tf_op jit(solution)/shard_map/all_gather | solution.py:125
  53.5 1.3 fusion.82
  54.8 1.1 fusion.81
  56.0 1.1 fusion.80
  57.1 1.1 convolution_add_fusion.47
  58.2 1.1 convolution_add_fusion.46
  59.4 1.1 convolution_add_fusion.45
  60.5 0.2 fusion.3
  61.2 0.2 convolution_add_fusion.41
  61.9 0.2 convolution_add_fusion.38
  63.1 0.2 convolution_add_fusion.33
  63.8 0.2 convolution_add_fusion.30
  64.2 0.2 convolution_add_fusion.28
  64.5 0.2 fusion.2
  65.2 0.3 fusion.37
  65.5 0.2 fusion.30
  65.7 0.2 fusion.29
  65.9 0.2 fusion.28
  66.2 0.2 fusion.27
  66.4 0.2 fusion.26
  66.6 0.2 fusion.25
  66.9 0.2 fusion.24
  67.1 0.2 fusion.23
  67.3 0.2 fusion.22
  67.6 0.2 fusion.21
  67.8 0.2 fusion.20
  68.0 0.2 fusion.19
  68.3 0.2 fusion.18
  68.5 0.2 fusion.17
  68.7 0.2 fusion.16
  68.9 0.2 fusion.15
  69.2 0.2 fusion.14
  69.4 0.2 fusion.13
  69.6 0.2 fusion.12
  69.9 0.2 fusion.11
  70.1 0.2 fusion.10
  70.3 0.2 fusion.9
  70.6 0.2 fusion.8
  70.8 0.2 fusion.7
  71.0 0.2 fusion.6
  71.3 0.2 fusion.5
  71.5 0.2 fusion.4
  71.7 3.4 %broadcast_multiply_fusion = f32[256,27,256]{2,0,1:T(8,128)} fusion(f32[256,27,256]{2,0,1:T(8,128)S(1)} %fusion.4), kind=kLoop, calls=%fused_computation | loop fusion | flops 1769472 | bytes 14155776 | tf_op jit(solution)/shard_map/mul | solution.py:105
  75.2 3.6 %collective-permute-start.2 = (bf16[1,1,8,8,256]{4,3,2,1,0:T(8,128)(2,1)S(1)}, bf16[1,1,8,8,256]{4,3,2,1,0:T(8,128)(2,1)S(1)}, u32[]{:S(2)}, u32[]{:S(2)}) collective-permute-start(bf16[1,1,8,8,256]{4,3,2,1,0:T(8,128)(2,1)S(1)} %get-tuple-element.3), channel_id=1, source_target_pairs={{0,2},{2,4},{4,6},{6,8},{8,10},{10,12},{12,14},{1,3},{3,5},{5,7},{... | collective-permute-start | bytes 98312 | tf_op jit(solution)/shard_map/ppermute | solution.py:15
  78.8 1.3 collective-permute-start.3
  80.1 0.7 fusion.79
  80.9 3.8 %collective-permute-done.3 = bf16[1,1,8,8,256]{4,3,2,1,0:T(8,128)(2,1)S(1)} collective-permute-done((bf16[1,1,8,8,256]{4,3,2,1,0:T(8,128)(2,1)S(1)}, bf16[1,1,8,8,256]{4,3,2,1,0:T(8,128)(2,1)S(1)}, u32[]{:S(2)}, u32[]{:S(2)}) %collective-permute-start.3) | collective-permute-done | bytes 32800 | tf_op jit(solution)/shard_map/ppermute | solution.py:17
  84.8 1.1 fusion.38
  85.9 1.1 fusion.42
  87.0 1.1 fusion.46
  88.1 1.1 convolution_add_fusion.23
  93.2 45.6 %reduce-scatter.2.cloned.1.call-done = f32[16,27,256]{2,0,1:T(8,128)} async-done(((f32[256,27,256]{2,0,1:T(8,128)}), f32[16,27,256]{2,0,1:T(8,128)}) %reduce-scatter.2.cloned.1.call-update) | async-done | bytes 442384 | tf_op jit(solution)/shard_map/reduce_scatter | solution.py:132
  138.9 1.1 convolution_add_fusion.2
  140.0 1.1 convolution_add_fusion.1
  141.1 1.8 fusion.32
  142.8 96.2 %all-reduce.4.cloned.1.call-done = f32[16,27,256]{2,0,1:T(8,128)} async-done(((f32[16,27,256]{2,0,1:T(8,128)}), f32[16,27,256]{2,0,1:T(8,128)}) %all-reduce.4.cloned.1.call-update) | async-done | bytes 442384 | tf_op jit(solution)/shard_map/psum | solution.py:133
  239.1 1.8 copy.87
  (49 shorter events, 7.1 us)
Async XLA Ops:
  7.2 53.3 %copy-start.2 = (bf16[1,4,8,8,256]{4,3,2,1,0:T(8,128)(2,1)S(1)}, bf16[1,4,8,8,256]{4,3,2,1,0:T(8,128)(2,1)}, u32[]{:S(2)}) copy-start(bf16[1,4,8,8,256]{4,3,2,1,0:T(8,128)(2,1)} %param.3) | copy-start | bytes 393220
  7.2 46.4 %all-gather.2.cloned.1.call-start = ((), (), s32[]{:S(2)}) async-start(), calls=%async_computation.1 | async-start | bytes 3760128 | tf_op jit(solution)/shard_map/all_gather | solution.py:125
  7.9 130.9 %reduce-scatter.2.cloned.1.call-start = ((), (), s32[]{:S(2)}) async-start(), calls=%async_computation.2 | async-start | bytes 7520256 | tf_op jit(solution)/shard_map/reduce_scatter | solution.py:132
  8.7 5.0 %collective-permute-start = (bf16[1,1,8,8,256]{4,3,2,1,0:T(8,128)(2,1)S(1)}, bf16[1,1,8,8,256]{4,3,2,1,0:T(8,128)(2,1)S(1)}, u32[]{:S(2)}, u32[]{:S(2)}) collective-permute-start(bf16[1,1,8,8,256]{4,3,2,1,0:T(8,128)(2,1)S(1)} %get-tuple-element.5), channel_id=1, source_target_pairs={{0,2},{2,4},{4,6},{6,8},{8,10},{10,12},{12,14},{1,3},{3,5},{5,7},{... | collective-permute-start | bytes 98312 | tf_op jit(solution)/shard_map/ppermute | solution.py:15
  12.1 5.8 %collective-permute-start.1 = (bf16[1,1,8,8,256]{4,3,2,1,0:T(8,128)(2,1)S(1)}, bf16[1,1,8,8,256]{4,3,2,1,0:T(8,128)(2,1)S(1)}, u32[]{:S(2)}, u32[]{:S(2)}) collective-permute-start(bf16[1,1,8,8,256]{4,3,2,1,0:T(8,128)(2,1)S(1)} %get-tuple-element.6), channel_id=1, source_target_pairs={{2,0},{4,2},{6,4},{8,6},{10,8},{12,10},{14,12},{3,1},{5,3},{7,5},{... | collective-permute-start | bytes 98312 | tf_op jit(solution)/shard_map/ppermute | solution.py:17
  53.5 7.0 %copy-start = (bf16[256,27,256]{2,0,1:T(8,128)(2,1)S(1)}, bf16[256,27,256]{2,0,1:T(8,128)(2,1)}, u32[]{:S(2)}) copy-start(bf16[256,27,256]{2,0,1:T(8,128)(2,1)} %all-gather.2.cloned.1.call-done) | copy-start | bytes 10616836
  63.1 2.1 copy-start.3
  75.1 163.9 %all-reduce.4.cloned.1.call-start = ((), (), s32[]{:S(2)}) async-start(), calls=%async_computation.3 | async-start | bytes 884736 | tf_op jit(solution)/shard_map/psum | solution.py:133
  75.2 14.1 %copy-start.1 = (bf16[256,27,256]{2,0,1:T(8,128)(2,1)S(1)}, bf16[256,27,256]{2,0,1:T(8,128)(2,1)}, u32[]{:S(2)}) copy-start(bf16[256,27,256]{2,0,1:T(8,128)(2,1)} %all-gather.2.cloned.1.call-done) | copy-start | bytes 10616836
  75.2 5.7 %collective-permute-start.2 = (bf16[1,1,8,8,256]{4,3,2,1,0:T(8,128)(2,1)S(1)}, bf16[1,1,8,8,256]{4,3,2,1,0:T(8,128)(2,1)S(1)}, u32[]{:S(2)}, u32[]{:S(2)}) collective-permute-start(bf16[1,1,8,8,256]{4,3,2,1,0:T(8,128)(2,1)S(1)} %get-tuple-element.3), channel_id=1, source_target_pairs={{0,2},{2,4},{4,6},{6,8},{8,10},{10,12},{12,14},{1,3},{3,5},{5,7},{... | collective-permute-start | bytes 98312 | tf_op jit(solution)/shard_map/ppermute | solution.py:15
  78.8 5.8 %collective-permute-start.3 = (bf16[1,1,8,8,256]{4,3,2,1,0:T(8,128)(2,1)S(1)}, bf16[1,1,8,8,256]{4,3,2,1,0:T(8,128)(2,1)S(1)}, u32[]{:S(2)}, u32[]{:S(2)}) collective-permute-start(bf16[1,1,8,8,256]{4,3,2,1,0:T(8,128)(2,1)S(1)} %get-tuple-element.4), channel_id=1, source_target_pairs={{2,0},{4,2},{6,4},{8,6},{10,8},{12,10},{14,12},{3,1},{5,3},{7,5},{... | collective-permute-start | bytes 98312 | tf_op jit(solution)/shard_map/ppermute | solution.py:17
Sparse Core Ops, SparseCore 0:
  9.9 43.6 all-gather.1
  75.2 63.5 reduce-scatter.1
  142.4 96.5 all-reduce.3
where the time goes:
time: 248 us; the launch traced here: 247 us
  waiting for transfers between devices  185 us (75%)
  matrix products  30 us (12%)
  between operations  14.4 us (6%)
  starting transfers between devices  9.72 us (4%)
  other arithmetic  5.36 us (2%)
  local copies, waits for them, and re-layouts  2.61 us (1%)
    psum x1, waiting for transfers between devices, local(): weight_grad = lax.psum(shard, ('slab', 'rep'))  96.2 us
    reduce_scatter x1, waiting for transfers between devices, local(): shard = lax.psum_scatter(terms, 'fsdp', scatter_dimension=0, tiled=True)  45.6 us
    all_gather x1, waiting for transfers between devices, local(): whole = lax.all_gather(weights, 'fsdp', axis=0, tiled=True)  34.5 us
    dot_general x27, matrix products, backward_rows(): jnp.einsum('bxyzo,oi->bxyzi', grad_window, weight_rows[:, index, :], pref...  12.2 us
    dot_general x27, matrix products, forward_rows(): jnp.einsum('bxyzi,oi->bxyzo', window, weight_rows[:, index, :], preferred...  11.7 us
    ppermute x2, waiting for transfers between devices, padded_2(): lax.ppermute(head, axis, [((i + 1) % count, i) for i in range(ends)])  8 us
    ppermute x2, starting transfers between devices, padded_2(): lax.ppermute(tail, axis, [(i, (i + 1) % count) for i in range(ends)])  7.02 us
    dot_general x27, matrix products, weight_terms(): jnp.einsum('bxyzo,bxyzi->oi', grads, window, preferred_element_type=jnp.f...  6.1 us
  transfers between devices with their start and end apart: 7, of which 6 were waited for; matrix products, arithmetic and copies ran while one was open for 6% of the time, Pallas kernels for 0%

commit v1 on v0

--- a/solution.py
+++ b/solution.py
@@ -130,7 +130,7 @@
     input_grad = backward_rows(grads_pad, whole).astype(jnp.bfloat16)
     terms = weight_terms(grad_pre, inputs_pad, factor)
     shard = lax.psum_scatter(terms, "fsdp", scatter_dimension=0, tiled=True)
-    weight_grad = lax.psum(shard, ("slab", "rep"))
+    weight_grad = jnp.sum(lax.all_gather(shard, ("slab", "rep")), axis=0)
     return (activated, input_grad, weight_grad)
 
 

time: 248 us -> 316 us (1.27)
  waiting for transfers between devices: 185 us -> 253 us
  other arithmetic: 5.36 us -> 11.9 us
  matrix products: 30 us -> 24.3 us
    all_gather x0 -> x1, waiting for transfers between devices: none -> 147 us  [local(): weight_grad = jnp.sum(lax.all_gather(shard, ('slab', 'rep')), axis=0)]
    psum x1 -> x0, waiting for transfers between devices: 96.2 us -> none  [local(): weight_grad = lax.psum(shard, ('slab', 'rep'))]
    reduce_scatter x1, waiting for transfers between devices: 45.6 us -> 63.6 us  [local(): shard = lax.psum_scatter(terms, 'fsdp', scatter_dimension=0, tiled=True)]
    dot_general x27, matrix products: 12.2 us -> 5.8 us  [backward_rows(): jnp.einsum('bxyzo,oi->bxyzi', grad_window, weight_rows[:, index, :], pref...]
    reduce_sum x0 -> x1, other arithmetic: none -> 4.69 us  [local(): weight_grad = jnp.sum(lax.all_gather(shard, ('slab', 'rep')), axis=0)]
  transfers between devices with their start and end apart: 7 -> 7, of which waited for: 6 -> 6; matrix products, arithmetic and copies ran while one was open for 6% -> 4% of each run, Pallas kernels for 0% -> 0%
where the time goes in v1:
time: 316 us; the launch traced here: 315 us
  waiting for transfers between devices  253 us (80%)
  matrix products  24.3 us (8%)
  between operations  14.4 us (5%)
  other arithmetic  11.9 us (4%)
  starting transfers between devices  9.48 us (3%)
    all_gather x1, waiting for transfers between devices, local(): weight_grad = jnp.sum(lax.all_gather(shard, ('slab', 'rep')), axis=0)  147 us
    reduce_scatter x1, waiting for transfers between devices, local(): shard = lax.psum_scatter(terms, 'fsdp', scatter_dimension=0, tiled=True)  63.6 us
    all_gather x1, waiting for transfers between devices, local(): whole = lax.all_gather(weights, 'fsdp', axis=0, tiled=True)  34.5 us
    dot_general x27, matrix products, forward_rows(): jnp.einsum('bxyzi,oi->bxyzo', window, weight_rows[:, index, :], preferred...  12.4 us
    ppermute x2, waiting for transfers between devices, padded_2(): lax.ppermute(head, axis, [((i + 1) % count, i) for i in range(ends)])  7.05 us
    ppermute x2, starting transfers between devices, padded_2(): lax.ppermute(tail, axis, [(i, (i + 1) % count) for i in range(ends)])  6.78 us
  transfers between devices with their start and end apart: 7, of which 6 were waited for; matrix products, arithmetic and copies ran while one was open for 4% of the time, Pallas kernels for 0%

profile of v1, /device:TPU:32, one launch (start us, length us, event | category | flops | bytes accessed | tf_op | source)
XLA Modules:
  0.0 315.0 jit_solution(1537251599530478516)
XLA Ops:
  7.2 0.7 all-gather.4.cloned.1.call-update
  8.0 0.8 fusion.94
  8.7 3.4 %collective-permute-start = (bf16[1,1,8,8,256]{4,3,2,1,0:T(8,128)(2,1)S(1)}, bf16[1,1,8,8,256]{4,3,2,1,0:T(8,128)(2,1)S(1)}, u32[]{:S(2)}, u32[]{:S(2)}) collective-permute-start(bf16[1,1,8,8,256]{4,3,2,1,0:T(8,128)(2,1)S(1)} %get-tuple-element.5), channel_id=1, source_target_pairs={{0,2},{2,4},{4,6},{6,8},{8,10},{10,12},{12,14},{1,3},{3,5},{5,7},{... | collective-permute-start | bytes 98312 | tf_op jit(solution)/shard_map/ppermute | solution.py:15
  12.1 1.3 collective-permute-start.1
  13.4 0.3 collective-permute-done
  13.7 4.2 %collective-permute-done.1 = bf16[1,1,8,8,256]{4,3,2,1,0:T(8,128)(2,1)S(1)} collective-permute-done((bf16[1,1,8,8,256]{4,3,2,1,0:T(8,128)(2,1)S(1)}, bf16[1,1,8,8,256]{4,3,2,1,0:T(8,128)(2,1)S(1)}, u32[]{:S(2)}, u32[]{:S(2)}) %collective-permute-start.1) | collective-permute-done | bytes 32800 | tf_op jit(solution)/shard_map/ppermute | solution.py:17
  17.9 1.1 select_maximum_fusion.2
  19.0 34.5 %all-gather.4.cloned.1.call-done = bf16[256,27,256]{2,0,1:T(8,128)(2,1)} async-done(((bf16[16,27,256]{2,0,1:T(8,128)(2,1)}), bf16[256,27,256]{2,0,1:T(8,128)(2,1)}) %all-gather.4.cloned.1.call-update) | async-done | bytes 3538960 | tf_op jit(solution)/shard_map/all_gather | solution.py:125
  53.5 1.3 fusion.82
  54.8 1.1 fusion.81
  56.0 1.1 fusion.80
  57.1 1.1 convolution_add_fusion.47
  58.2 1.1 convolution_add_fusion.46
  59.4 1.1 convolution_add_fusion.45
  60.5 0.2 fusion.3
  60.7 0.2 convolution_add_fusion.43
  61.2 0.2 convolution_add_fusion.41
  61.9 0.2 convolution_add_fusion.38
  62.8 0.2 convolution_add_fusion.34
  63.1 0.2 convolution_add_fusion.33
  63.8 0.2 convolution_add_fusion.30
  64.2 0.2 convolution_add_fusion.28
  64.5 0.2 fusion.2
  64.7 0.2 convolution_add_fusion.26
  64.9 0.2 convolution_add_fusion.25
  65.2 1.0 fusion.37
  66.1 0.2 fusion.30
  66.4 0.2 fusion.29
  66.6 0.2 fusion.28
  66.8 0.2 fusion.27
  67.1 0.2 fusion.26
  67.3 0.2 fusion.25
  67.5 0.2 fusion.24
  67.8 0.2 fusion.23
  68.0 0.2 fusion.22
  68.2 0.2 fusion.21
  68.5 0.2 fusion.20
  68.7 0.2 fusion.19
  68.9 0.2 fusion.18
  69.2 0.2 fusion.17
  69.4 0.2 fusion.16
  69.6 0.2 fusion.15
  69.9 0.2 fusion.14
  70.1 0.2 fusion.13
  70.3 0.2 fusion.12
  70.6 0.2 fusion.11
  70.8 0.2 fusion.10
  71.0 0.2 fusion.9
  71.3 0.2 fusion.8
  71.5 0.2 fusion.7
  71.7 0.2 fusion.6
  72.0 0.2 fusion.5
  72.2 0.2 fusion.4
  72.4 3.4 %broadcast_multiply_fusion = f32[256,27,256]{2,0,1:T(8,128)} fusion(f32[256,27,256]{2,0,1:T(8,128)S(1)} %fusion.4), kind=kLoop, calls=%fused_computation | loop fusion | flops 1769472 | bytes 14155776 | tf_op jit(solution)/shard_map/mul | solution.py:105
  75.9 63.6 %reduce-scatter.2.cloned.1.call-done = f32[16,27,256]{2,0,1:T(8,128)} async-done(((f32[256,27,256]{2,0,1:T(8,128)}), f32[16,27,256]{2,0,1:T(8,128)}) %reduce-scatter.2.cloned.1.call-update) | async-done | bytes 442384 | tf_op jit(solution)/shard_map/reduce_scatter | solution.py:132
  139.5 0.8 fusion.93
  140.3 3.4 %collective-permute-start.2 = (bf16[1,1,8,8,256]{4,3,2,1,0:T(8,128)(2,1)S(1)}, bf16[1,1,8,8,256]{4,3,2,1,0:T(8,128)(2,1)S(1)}, u32[]{:S(2)}, u32[]{:S(2)}) collective-permute-start(bf16[1,1,8,8,256]{4,3,2,1,0:T(8,128)(2,1)S(1)} %get-tuple-element.3), channel_id=1, source_target_pairs={{0,2},{2,4},{4,6},{6,8},{8,10},{10,12},{12,14},{1,3},{3,5},{5,7},{... | collective-permute-start | bytes 98312 | tf_op jit(solution)/shard_map/ppermute | solution.py:15
  143.7 1.3 collective-permute-start.3
  145.0 1.7 fusion.79
  146.7 2.8 collective-permute-done.3
  149.6 1.1 select_maximum_fusion
  155.8 0.8 fusion.32
  156.7 147.1 %all-gather.6.cloned.1.call-done = f32[256,27,256]{2,0,1:T(8,128)} async-done(((f32[16,27,256]{2,0,1:T(8,128)}), f32[256,27,256]{2,0,1:T(8,128)}) %all-gather.6.cloned.1.call-update) | async-done | bytes 7077904 | tf_op jit(solution)/shard_map/all_gather | solution.py:133
  303.7 4.7 %reduce_sum.9 = f32[16,27,256]{2,0,1:T(8,128)} reduce(f32[16,16,27,256]{3,1,0,2:T(8,128)} %bitcast.689, f32[]{:T(128)} %constant.10.clone.1), dimensions={0}, to_apply=%region_1.2 | reduce | flops 1658880 | bytes 7520260 | tf_op jit(solution)/shard_map/reduce_sum | solution.py:133
  (53 shorter events, 7.1 us)
Async XLA Ops:
  7.2 53.3 %copy-start.2 = (bf16[1,4,8,8,256]{4,3,2,1,0:T(8,128)(2,1)S(1)}, bf16[1,4,8,8,256]{4,3,2,1,0:T(8,128)(2,1)}, u32[]{:S(2)}) copy-start(bf16[1,4,8,8,256]{4,3,2,1,0:T(8,128)(2,1)} %param.3) | copy-start | bytes 393220
  7.2 46.4 %all-gather.4.cloned.1.call-start = ((), (), s32[]{:S(2)}) async-start(), calls=%async_computation.1 | async-start | bytes 3760128 | tf_op jit(solution)/shard_map/all_gather | solution.py:125
  7.9 131.6 %reduce-scatter.2.cloned.1.call-start = ((), (), s32[]{:S(2)}) async-start(), calls=%async_computation.2 | async-start | bytes 7520256 | tf_op jit(solution)/shard_map/reduce_scatter | solution.py:132
  8.7 5.0 %collective-permute-start = (bf16[1,1,8,8,256]{4,3,2,1,0:T(8,128)(2,1)S(1)}, bf16[1,1,8,8,256]{4,3,2,1,0:T(8,128)(2,1)S(1)}, u32[]{:S(2)}, u32[]{:S(2)}) collective-permute-start(bf16[1,1,8,8,256]{4,3,2,1,0:T(8,128)(2,1)S(1)} %get-tuple-element.5), channel_id=1, source_target_pairs={{0,2},{2,4},{4,6},{6,8},{8,10},{10,12},{12,14},{1,3},{3,5},{5,7},{... | collective-permute-start | bytes 98312 | tf_op jit(solution)/shard_map/ppermute | solution.py:15
  12.1 5.8 %collective-permute-start.1 = (bf16[1,1,8,8,256]{4,3,2,1,0:T(8,128)(2,1)S(1)}, bf16[1,1,8,8,256]{4,3,2,1,0:T(8,128)(2,1)S(1)}, u32[]{:S(2)}, u32[]{:S(2)}) collective-permute-start(bf16[1,1,8,8,256]{4,3,2,1,0:T(8,128)(2,1)S(1)} %get-tuple-element.6), channel_id=1, source_target_pairs={{2,0},{4,2},{6,4},{8,6},{10,8},{12,10},{14,12},{3,1},{5,3},{7,5},{... | collective-permute-start | bytes 98312 | tf_op jit(solution)/shard_map/ppermute | solution.py:17
  53.5 7.0 %copy-start = (bf16[256,27,256]{2,0,1:T(8,128)(2,1)S(1)}, bf16[256,27,256]{2,0,1:T(8,128)(2,1)}, u32[]{:S(2)}) copy-start(bf16[256,27,256]{2,0,1:T(8,128)(2,1)} %all-gather.4.cloned.1.call-done) | copy-start | bytes 10616836
  63.1 2.1 copy-start.5
  66.1 6.0 %copy-start.3 = (bf16[1,4,8,8,256]{4,3,2,1,0:T(8,128)(2,1)}, bf16[1,4,8,8,256]{4,3,2,1,0:T(8,128)(2,1)S(1)}, u32[]{:S(2)}) copy-start(bf16[1,4,8,8,256]{4,3,2,1,0:T(8,128)(2,1)S(1)} %get-tuple-element.7) | copy-start | bytes 393220
  75.8 74.8 %copy-start.1 = (bf16[256,27,256]{2,0,1:T(8,128)(2,1)S(1)}, bf16[256,27,256]{2,0,1:T(8,128)(2,1)}, u32[]{:S(2)}) copy-start(bf16[256,27,256]{2,0,1:T(8,128)(2,1)} %all-gather.4.cloned.1.call-done) | copy-start | bytes 10616836
  75.8 227.9 %all-gather.6.cloned.1.call-start = ((), (), s32[]{:S(2)}) async-start(), calls=%async_computation.3 | async-start | bytes 7520256 | tf_op jit(solution)/shard_map/all_gather | solution.py:133
  139.5 12.3 %copy-start.4 = (bf16[1,4,8,8,256]{4,3,2,1,0:T(8,128)(2,1)S(1)}, bf16[1,4,8,8,256]{4,3,2,1,0:T(8,128)(2,1)}, u32[]{:S(2)}) copy-start(bf16[1,4,8,8,256]{4,3,2,1,0:T(8,128)(2,1)} %copy-done.3) | copy-start | bytes 393220
  140.3 6.4 %collective-permute-start.2 = (bf16[1,1,8,8,256]{4,3,2,1,0:T(8,128)(2,1)S(1)}, bf16[1,1,8,8,256]{4,3,2,1,0:T(8,128)(2,1)S(1)}, u32[]{:S(2)}, u32[]{:S(2)}) collective-permute-start(bf16[1,1,8,8,256]{4,3,2,1,0:T(8,128)(2,1)S(1)} %get-tuple-element.3), channel_id=1, source_target_pairs={{0,2},{2,4},{4,6},{6,8},{8,10},{10,12},{12,14},{1,3},{3,5},{5,7},{... | collective-permute-start | bytes 98312 | tf_op jit(solution)/shard_map/ppermute | solution.py:15
  143.7 5.8 %collective-permute-start.3 = (bf16[1,1,8,8,256]{4,3,2,1,0:T(8,128)(2,1)S(1)}, bf16[1,1,8,8,256]{4,3,2,1,0:T(8,128)(2,1)S(1)}, u32[]{:S(2)}, u32[]{:S(2)}) collective-permute-start(bf16[1,1,8,8,256]{4,3,2,1,0:T(8,128)(2,1)S(1)} %get-tuple-element.4), channel_id=1, source_target_pairs={{2,0},{4,2},{6,4},{8,6},{10,8},{12,10},{14,12},{3,1},{5,3},{7,5},{... | collective-permute-start | bytes 98312 | tf_op jit(solution)/shard_map/ppermute | solution.py:17
Sparse Core Ops, SparseCore 0:
  9.9 43.6 all-gather.3
  75.9 63.4 reduce-scatter.1
  141.4 162.2 all-gather.5
